TPU v7x, 768 devices: a whole 4x8x12 slice. The times are simulated.
768 devices in a mesh: row: 16 (over z_hi, x), col: 8 (over y), depth: 6 (over z_lo, core).
Axes of the slice: x: 4, y: 8, z: 12 (z_hi: 4, z_lo: 3; z = z_hi * 3 + z_lo), core: 2. Of those that a mesh axis runs over, the one named last changes fastest.
Arguments:
- left_panels: bfloat16 [8192, 6, 2048], P('row', 'depth', 'col'), may hold values from -6 to 6
- right_panels: bfloat16 [6, 2048, 6144], P('depth', 'row', 'col'), may hold values from -0.0546875 to 0.0546875
- left_flags: int32 [64, 6, 16], P('row', 'depth', 'col'), may hold values from 0 to 1, as said below
- right_flags: int32 [6, 16, 48], P('depth', 'row', 'col'), may hold values 0 or 1
- target_flags: int32 [64, 48], P('row', ('col', 'depth')), may hold values 0 or 1
Outputs:
- product: bfloat16 [8192, 6144], P('row', ('col', 'depth'))
Inputs may be any that keep to these rules, and one draw needn't show every extreme that they name: `left_flags`: 1 where the block is stored, else 0.
All inputs are finite; a program needn't handle non-finite values. No bound on the sum of `right_flags` or of `target_flags` on one device may be relied on, other than what follows from the above.
Results may differ from a plain program's by a relative error of at most 0.001.
Values may be sent and summed in bfloat16 or wider, within the bound.
A program may use at most 32 MiB of HBM per device.

v0:
```python
import jax
import jax.numpy as jnp
from jax import lax
from jax.sharding import PartitionSpec as P

BLOCK = 128


def spread(occupancy, out_type):
    height, breadth = occupancy.shape
    expanded = jnp.broadcast_to(occupancy[:, None, :, None], (height, BLOCK, breadth, BLOCK))
    return expanded.reshape(height * BLOCK, breadth * BLOCK).astype(out_type)


def on_device(left_panels, right_panels, left_flags, right_flags, target_flags):
    left_masked = left_panels[:, 0, :] * spread(left_flags[:, 0, :], jnp.bfloat16)
    right_masked = right_panels[0] * spread(right_flags[0], jnp.bfloat16)
    gathered_right = lax.all_gather(right_masked, "row", axis=0, tiled=True)
    partial_value = jnp.dot(
        lax.all_gather(left_masked, "col", axis=1, tiled=True),
        gathered_right,
        preferred_element_type=jnp.float32,
    )
    summed = lax.psum_scatter(partial_value, "depth", scatter_dimension=1, tiled=True)
    return (summed * spread(target_flags, jnp.float32)).astype(jnp.bfloat16)


def solution(mesh):
    in_specs = (
        P("row", "depth", "col"),
        P("depth", "row", "col"),
        P("row", "depth", "col"),
        P("depth", "row", "col"),
        P("row", ("col", "depth")),
    )
    out_specs = P("row", ("col", "depth"))
    return jax.shard_map(
        on_device, mesh=mesh, in_specs=in_specs, out_specs=out_specs, check_vma=False
    )
```

profile of v0, /device:TPU:1, one launch (start us, length us, event | category | flops | bytes accessed | tf_op | source)
XLA Modules:
  0.0 216.1 jit_solution(10759253184022757797)
XLA Ops:
  6.5 0.0 all-gather.3.cloned.1.call-start
  6.5 0.7 convert_bitcast_fusion.2
  7.2 0.1 copy.6
  7.3 0.2 broadcast_in_dim.20
  7.5 1.7 bitcast_multiply_fusion
  9.2 0.0 all-gather.3.cloned.1.call-update
  9.3 0.0 all-gather.5.cloned.1.call-start
  9.3 0.7 convert_bitcast_fusion.1
  10.0 0.1 broadcast_bitcast_fusion.1
  10.1 1.6 bitcast_multiply_fusion.1
  11.7 0.0 all-gather.5.cloned.1.call-update
  11.7 0.0 copy-start
  11.7 0.0 reduce-scatter.2.cloned.1.call-start
  11.8 54.1 %all-gather.3.cloned.1.call-done = bf16[512,2048]{1,0:T(8,128)(2,1)} async-done(((bf16[512,256]{1,0:T(8,128)(2,1)}), bf16[512,2048]{1,0:T(8,128)(2,1)}) %all-gather.3.cloned.1.call-update) | async-done | bytes 2097168 | tf_op jit(solution)/shard_map/all_gather | solution.py:20
  65.9 103.8 %all-gather.5.cloned.1.call-done = bf16[2048,768]{1,0:T(8,128)(2,1)} async-done(((bf16[128,768]{1,0:T(8,128)(2,1)}), bf16[2048,768]{1,0:T(8,128)(2,1)}) %all-gather.5.cloned.1.call-update) | async-done | bytes 3145744 | tf_op jit(solution)/shard_map/all_gather | solution.py:18
  169.7 5.5 %fusion = f32[512,768]{1,0:T(8,128)} fusion(bf16[512,2048]{1,0:T(8,128)(2,1)} %all-gather.3.cloned.1.call-done, bf16[2048,768]{1,0:T(8,128)(2,1)} %all-gather.5.cloned.1.call-done), kind=kOutput, calls=%fused_computation.8 | convolution fusion | flops 1610612736 | bytes 6815744 | tf_op jit(solution)/shard_map/dot_general | solution.py:19
  175.2 0.0 reduce-scatter.2.cloned.1.call-update
  175.2 0.0 copy-done
  175.3 0.1 broadcast_bitcast_fusion
  175.3 32.5 %reduce-scatter.2.cloned.1.call-done = f32[512,128]{1,0:T(8,128)} async-done(((f32[512,768]{1,0:T(8,128)}), f32[512,128]{1,0:T(8,128)}) %reduce-scatter.2.cloned.1.call-update) | async-done | bytes 262160 | tf_op jit(solution)/shard_map/reduce_scatter | solution.py:24
  207.9 1.7 multiply_convert_fusion
  (1 shorter events, 0.0 us)
Async XLA Ops:
  6.5 59.4 %all-gather.3.cloned.1.call-start = ((), (), s32[]{:S(2)}) async-start(), calls=%async_computation.1 | async-start | bytes 2359296 | tf_op jit(solution)/shard_map/all_gather | solution.py:20
  9.3 160.4 %all-gather.5.cloned.1.call-start = ((), (), s32[]{:S(2)}) async-start(), calls=%async_computation.2 | async-start | bytes 3342336 | tf_op jit(solution)/shard_map/all_gather | solution.py:18
  11.7 163.5 %copy-start = (s32[4,1]{0,1:T(1,128)S(1)}, s32[4,1]{0,1:T(1,128)}, u32[]{:S(2)}) copy-start(s32[4,1]{0,1:T(1,128)} %param.9) | copy-start | bytes 52
  11.7 196.2 %reduce-scatter.2.cloned.1.call-start = ((), (), s32[]{:S(2)}) async-start(), calls=%async_computation.3 | async-start | bytes 1835008 | tf_op jit(solution)/shard_map/reduce_scatter | solution.py:24
Sparse Core Ops, SparseCore 0:
  9.7 56.1 all-gather.2
  69.5 100.1 all-gather.4
  175.4 32.4 reduce-scatter.1
where the time goes:
time: 218 us; the launch traced here: 216 us
  waiting for transfers between devices  191 us (88%)
  between operations  13.1 us (6%)
  other arithmetic  6.42 us (3%)
  matrix products  5.53 us (3%)
    all_gather x1, waiting for transfers between devices, on_device(): gathered_right = lax.all_gather(right_masked, 'row', axis=0, tiled=True)  104 us
    all_gather x1, waiting for transfers between devices, on_device(): lax.all_gather(left_masked, 'col', axis=1, tiled=True)  54.1 us
    reduce_scatter x1, waiting for transfers between devices, on_device(): lax.psum_scatter(partial_value, 'depth', scatter_dimension=1, tiled=True)  32.5 us
    dot_general x1, matrix products, on_device(): jnp.dot(lax.all_gather(left_masked, 'col', axis=1, tiled=True), gathered_...  5.53 us
  transfers between devices with their start and end apart: 3, of which 3 were waited for; matrix products, arithmetic and copies ran while one was open for 1% of the time, Pallas kernels for 0%

commit v1 on v0

v1 whole, which is shorter than its diff:
```python
import jax
import jax.numpy as jnp
from jax import lax
from jax.experimental import pallas as pl
from jax.experimental.pallas import tpu as pltpu
from jax.sharding import PartitionSpec as P

BLOCK = 128
MESH = pl.DeviceIdType.MESH
NX, NY, NZH, NZL = 4, 8, 4, 3
HALF = 256
WIDE = 256
CHUNKS = 3


def kernel(
    left_hbm, right_hbm, left_flags, right_flags, target_flags, out_ref,
    left_in, right_in, left_buf, right_buf, part, sib_recv, red_send, red_recv,
    in_sem, left_send, left_recv, z_send, z_recv, x_send, x_recv,
    sib_send_sem, sib_recv_sem, red_send_sem, red_recv_sem,
):
    row, col, depth = lax.axis_index("row"), lax.axis_index("col"), lax.axis_index("depth")
    zh, x = row // NX, row % NX
    zl, core = depth // 2, depth % 2
    sign = 1 - 2 * core

    def y_id(step):
        return (row, (col + step * sign + NY) % NY, depth)

    def x_id(step):
        return (zh * NX + (x + step * sign + NX) % NX, col, depth)

    def z_id(step):
        return (((zh + step * sign + NZH) % NZH) * NX + x, col, depth)

    def layer_id(step):
        return (row, col, ((zl + step) % NZL) * 2 + core)

    sibling = (row, col, zl * 2 + 1 - core)

    left_copy = pltpu.make_async_copy(left_hbm, left_in, in_sem.at[0])
    right_copy = pltpu.make_async_copy(right_hbm, right_in, in_sem.at[1])
    left_copy.start()
    right_copy.start()

    barrier = pltpu.get_barrier_semaphore()
    friends = [y_id(1), y_id(-1), x_id(1), x_id(-1), z_id(1), z_id(-1), layer_id(1), layer_id(2), sibling]
    for friend in friends:
        pl.semaphore_signal(barrier, inc=1, device_id=friend, device_id_type=MESH)

    def chunk_of(step):
        return (zl + 1 + step) % NZL

    def mask_left(half):
        for block in range(2):
            rows = pl.ds(half * HALF + block * BLOCK, BLOCK)
            for k in range(2):
                columns = pl.ds(k * BLOCK, BLOCK)
                keep = left_flags[k, half * 2 + block] > 0
                value = left_in[rows, columns]
                left_buf[col, rows, columns] = jnp.where(keep, value, jnp.zeros_like(value))

    def mask_right(step):
        chunk = chunk_of(step)
        for j in range(2):
            keep = right_flags[0, chunk * 2 + j] > 0
            start = pl.multiple_of(chunk * WIDE + j * BLOCK, BLOCK)
            value = right_in[:, pl.ds(start, BLOCK)]
            right_buf[step, row, :, pl.ds(j * BLOCK, BLOCK)] = jnp.where(keep, value, jnp.zeros_like(value))

    pending = []

    def send(ref, send_sem, recv_sem, target):
        copy = pltpu.make_async_remote_copy(
            src_ref=ref, dst_ref=ref, send_sem=send_sem, recv_sem=recv_sem,
            device_id=target, device_id_type=MESH,
        )
        copy.start()
        pending.append(copy)

    def arrived(ref, send_sem, recv_sem, target):
        pltpu.make_async_remote_copy(
            src_ref=ref, dst_ref=ref, send_sem=send_sem, recv_sem=recv_sem,
            device_id=target, device_id_type=MESH,
        ).wait_recv()

    def left_ref(hop, way, half):
        shift = -hop * sign if way == 0 else hop * sign
        return left_buf.at[(col + shift + NY) % NY, pl.ds(half * HALF, HALF), :]

    def left_send_hop(hop, way, half):
        send(left_ref(hop - 1, way, half), left_send.at[hop - 1, way, half],
             left_recv.at[hop - 1, way, half], y_id(1 if way == 0 else -1))

    def left_wait(hop, way, half):
        arrived(left_ref(hop, way, half), left_send.at[hop - 1, way, half],
                left_recv.at[hop - 1, way, half], y_id(1 if way == 0 else -1))

    def left_event(hop, half):
        left_wait(hop, 0, half)
        if hop < 4:
            left_send_hop(hop + 1, 0, half)
        if hop < 4:
            left_wait(hop, 1, half)
            if hop < 3:
                left_send_hop(hop + 1, 1, half)

    def zh_of(kind):
        shift = (0, -sign, sign, 2)[kind]
        return (zh + shift + NZH) % NZH

    def z_ref(step, kind):
        return right_buf.at[step, zh_of(kind) * NX + x]

    def z_start(step):
        send(z_ref(step, 0), z_send.at[step, 0], z_recv.at[step, 0], z_id(1))
        send(z_ref(step, 0), z_send.at[step, 1], z_recv.at[step, 1], z_id(-1))

    def z_first(step):
        arrived(z_ref(step, 1), z_send.at[step, 0], z_recv.at[step, 0], z_id(1))
        send(z_ref(step, 1), z_send.at[step, 2], z_recv.at[step, 2], z_id(1))
        x_start(step, 1)
        arrived(z_ref(step, 2), z_send.at[step, 1], z_recv.at[step, 1], z_id(-1))
        x_start(step, 2)

    def z_second(step):
        arrived(z_ref(step, 3), z_send.at[step, 2], z_recv.at[step, 2], z_id(1))
        x_start(step, 3)

    def x_ref(step, kind, shift):
        return right_buf.at[step, zh_of(kind) * NX + (x + shift * sign + NX) % NX]

    def x_start(step, kind):
        send(x_ref(step, kind, 0), x_send.at[step, kind, 0], x_recv.at[step, kind, 0], x_id(1))
        send(x_ref(step, kind, 0), x_send.at[step, kind, 1], x_recv.at[step, kind, 1], x_id(-1))

    def x_first(step, kind):
        arrived(x_ref(step, kind, -1), x_send.at[step, kind, 0], x_recv.at[step, kind, 0], x_id(1))
        send(x_ref(step, kind, -1), x_send.at[step, kind, 2], x_recv.at[step, kind, 2], x_id(1))

    def x_last(step):
        for kind in range(4):
            arrived(x_ref(step, kind, 1), x_send.at[step, kind, 1], x_recv.at[step, kind, 1], x_id(-1))
        for kind in range(4):
            arrived(x_ref(step, kind, 2), x_send.at[step, kind, 2], x_recv.at[step, kind, 2], x_id(1))

    def multiply(step):
        total = None
        for k in range(NY):
            term = jnp.dot(
                left_buf[k], right_buf[step, 2 * k:2 * k + 2].reshape(2 * BLOCK, WIDE),
                preferred_element_type=jnp.float32,
            )
            total = term if total is None else total + term
        part[step, 0] = total[:, :BLOCK]
        part[step, 1] = total[:, BLOCK:]
        copy = pltpu.make_async_remote_copy(
            src_ref=part.at[step, 1 - core], dst_ref=sib_recv.at[step],
            send_sem=sib_send_sem.at[step], recv_sem=sib_recv_sem.at[step],
            device_id=sibling, device_id_type=MESH,
        )
        copy.start()
        pending.append(copy)
        return copy

    def reduce_send(step, copy):
        copy.wait_recv()
        red_send[step] = part[step, core] + sib_recv[step]
        copy = pltpu.make_async_remote_copy(
            src_ref=red_send.at[step], dst_ref=red_recv.at[step],
            send_sem=red_send_sem.at[step], recv_sem=red_recv_sem.at[step],
            device_id=layer_id(1 + step), device_id_type=MESH,
        )
        copy.start()
        pending.append(copy)
        return copy

    right_copy.wait()
    mask_right(0)
    left_copy.wait()
    mask_left(0)
    pl.semaphore_wait(barrier, len(friends))
    z_start(0)
    x_start(0, 0)
    left_send_hop(1, 0, 0)
    left_send_hop(1, 1, 0)
    mask_left(1)
    left_send_hop(1, 0, 1)
    left_send_hop(1, 1, 1)
    mask_right(1)
    z_start(1)
    x_start(1, 0)
    mask_right(2)
    x_start(2, 0)

    x_first(0, 0)
    left_event(1, 0)
    z_first(0)
    z_start(2)
    x_first(1, 0)
    x_first(2, 0)
    left_event(1, 1)
    x_first(0, 1)
    x_first(0, 2)
    left_event(2, 0)
    z_first(1)
    z_second(0)
    left_event(2, 1)
    x_first(1, 1)
    x_first(1, 2)
    x_first(0, 3)
    left_event(3, 0)
    z_first(2)
    left_event(3, 1)
    z_second(1)
    x_first(2, 1)
    x_first(2, 2)
    x_first(1, 3)
    z_second(2)
    left_event(4, 0)
    left_event(4, 1)
    x_last(0)
    first = multiply(0)
    x_first(2, 3)
    red0 = reduce_send(0, first)
    x_last(1)
    second = multiply(1)
    red1 = reduce_send(1, second)
    x_last(2)
    third = multiply(2)
    third.wait_recv()
    total = part[2, core] + sib_recv[2]
    red0.wait_recv()
    red1.wait_recv()
    total = total + red_recv[0] + red_recv[1]
    for block in range(4):
        rows = slice(block * BLOCK, (block + 1) * BLOCK)
        keep = target_flags[0, block] > 0
        value = total[rows]
        out_ref[rows, :] = jnp.where(keep, value, jnp.zeros_like(value)).astype(jnp.bfloat16)
    for copy in pending:
        copy.wait_send()


def on_device(left_panels, right_panels, left_flags, right_flags, target_flags):
    dma = pltpu.SemaphoreType.DMA
    return pl.pallas_call(
        kernel,
        out_shape=jax.ShapeDtypeStruct((4 * BLOCK, BLOCK), jnp.bfloat16),
        in_specs=[pl.BlockSpec(memory_space=pl.ANY)] * 2 + [pl.BlockSpec(memory_space=pltpu.SMEM)] * 3,
        out_specs=pl.BlockSpec(memory_space=pltpu.VMEM),
        scratch_shapes=[
            pltpu.VMEM((4 * BLOCK, 2 * BLOCK), jnp.bfloat16),
            pltpu.VMEM((BLOCK, 6 * BLOCK), jnp.bfloat16),
            pltpu.VMEM((NY, 4 * BLOCK, 2 * BLOCK), jnp.bfloat16),
            pltpu.VMEM((CHUNKS, NX * NZH, BLOCK, WIDE), jnp.bfloat16),
            pltpu.VMEM((CHUNKS, 2, 4 * BLOCK, BLOCK), jnp.float32),
            pltpu.VMEM((CHUNKS, 4 * BLOCK, BLOCK), jnp.float32),
            pltpu.VMEM((2, 4 * BLOCK, BLOCK), jnp.float32),
            pltpu.VMEM((2, 4 * BLOCK, BLOCK), jnp.float32),
            dma((2,)),
            dma((4, 2, 2)),
            dma((4, 2, 2)),
            dma((CHUNKS, 3)),
            dma((CHUNKS, 3)),
            dma((CHUNKS, 4, 3)),
            dma((CHUNKS, 4, 3)),
            dma((CHUNKS,)),
            dma((CHUNKS,)),
            dma((2,)),
            dma((2,)),
        ],
        compiler_params=pltpu.CompilerParams(
            collective_id=0, has_side_effects=True, vmem_limit_bytes=32 * 1024 * 1024
        ),
        cost_estimate=pl.CostEstimate(flops=1_610_612_736, bytes_accessed=600_000, transcendentals=0),
    )(left_panels[:, 0, :], right_panels[0], left_flags[:, 0, :].T, right_flags[0], target_flags.T)


def solution(mesh):
    in_specs = (
        P("row", "depth", "col"),
        P("depth", "row", "col"),
        P("row", "depth", "col"),
        P("depth", "row", "col"),
        P("row", ("col", "depth")),
    )
    out_specs = P("row", ("col", "depth"))
    return jax.shard_map(
        on_device, mesh=mesh, in_specs=in_specs, out_specs=out_specs, check_vma=False
    )
```

time: 218 us -> 68 us (0.31)
  waiting for transfers between devices: 191 us -> 0 us
  Pallas kernels: 0 us -> 64.6 us
  between operations: 13.1 us -> 0.02 us
  other arithmetic: 6.42 us -> 0 us
  matrix products: 5.53 us -> 0 us
  local copies, waits for them, and re-layouts: 0.47 us -> 3.23 us
    all_gather x2 -> x0, waiting for transfers between devices: 158 us -> none  [the longest x1 104 us: on_device(): gathered_right = lax.all_gather(right_masked, 'row', axis=0, tiled=True)]
    pallas_call x0 -> x1, Pallas kernels: none -> 64.6 us  [on_device(): pl.pallas_call(kernel, out_shape=jax.ShapeDtypeStruct((4 * BLOCK, BLOCK),...]
    reduce_scatter x1 -> x0, waiting for transfers between devices: 32.5 us -> none  [on_device(): lax.psum_scatter(partial_value, 'depth', scatter_dimension=1, tiled=True)]
    dot_general x1 -> x0, matrix products: 5.53 us -> none  [on_device(): jnp.dot(lax.all_gather(left_masked, 'col', axis=1, tiled=True), gathered_...]
    mul x2 -> x0, other arithmetic: 3.33 us -> none  [the longest x1 1.7 us: on_device(): left_panels[:, 0, :] * spread(left_flags[:, 0, :], jnp.bfloat16)]
    unnamed x2 -> x11, local copies, waits for them, and re-layouts: 0.01 us -> 3.23 us
    convert_element_type x4 -> x0, other arithmetic: 3.09 us -> none  [the longest x1 1.74 us: on_device(): return (summed * spread(target_flags, jnp.float32)).astype(jnp.bfloat16)]
  transfers between devices with their start and end apart: 3 -> 0, of which waited for: 3 -> 0; matrix products, arithmetic and copies ran while one was open for 1% -> 0% of each run, Pallas kernels for 0% -> 0%
where the time goes in v1:
time: 68 us; the launch traced here: 67.8 us
  Pallas kernels  64.6 us (95%)
  local copies, waits for them, and re-layouts  3.23 us (5%)
    pallas_call x1, Pallas kernels, on_device(): pl.pallas_call(kernel, out_shape=jax.ShapeDtypeStruct((4 * BLOCK, BLOCK),...  64.6 us
    unnamed x11, local copies, waits for them, and re-layouts  3.23 us

profile of v1, /device:TPU:1, one launch (start us, length us, event | category | flops | bytes accessed | tf_op | source)
XLA Modules:
  0.0 67.8 jit_solution(13386134788525495375)
XLA Ops:
  0.0 0.0 copy-start.4
  0.0 0.0 copy-start.2
  0.0 0.0 copy-start.3
  0.0 0.6 copy-done.4
  0.7 0.0 copy-done.2
  0.7 0.0 copy-done.3
  0.7 0.0 copy-start
  0.7 0.9 %copy-done = bf16[512,1,256]{2,0,1:T(8,128)(2,1)S(1)} copy-done((bf16[512,1,256]{2,0,1:T(8,128)(2,1)S(1)}, bf16[512,1,256]{2,0,1:T(8,128)(2,1)}, u32[]{:S(2)}) %copy-start) | copy-done | bytes 262168
  1.6 0.0 copy-start.1
  1.7 0.9 %copy-done.1 = bf16[1,128,768]{2,1,0:T(8,128)(2,1)S(1)} copy-done((bf16[1,128,768]{2,1,0:T(8,128)(2,1)S(1)}, bf16[1,128,768]{2,1,0:T(8,128)(2,1)}, u32[]{:S(2)}) %copy-start.1) | copy-done | bytes 196632
  2.6 64.6 %shard_map.55 = bf16[512,128]{1,0:T(8,128)(2,1)S(1)} custom-call(bf16[512,256]{1,0:T(8,128)(2,1)S(1)} %bitcast.7, bf16[128,768]{1,0:T(8,128)(2,1)S(1)} %bitcast.8, s32[2,4]{1,0:T(2,128)S(1)} %bitcast.9, s32[1,6]{1,0:T(1,128)S(1)} %bitcast.10, s32[1,4]{1,0:T(1,128)S(1)} %bitcast.11), custom_call_target="tpu_custom_call" | custom-call | flops 1610612736 | bytes 600000 | tf_op jit(solution)/shard_map/pallas_call | solution.py:247
  67.2 0.7 copy.7
Async XLA Ops:
  0.0 0.7 copy-start.4
  0.0 0.7 %copy-start.2 = (s32[4,1,2]{0,2,1:T(2,128)S(1)}, s32[4,1,2]{0,2,1:T(2,128)}, u32[]{:S(2)}) copy-start(s32[4,1,2]{0,2,1:T(2,128)} %param.7) | copy-start | bytes 100
  0.0 0.7 %copy-start.3 = (s32[1,1,6]{2,1,0:T(1,128)S(1)}, s32[1,1,6]{2,1,0:T(1,128)}, u32[]{:S(2)}) copy-start(s32[1,1,6]{2,1,0:T(1,128)} %param.8) | copy-start | bytes 76
  0.7 1.0 %copy-start = (bf16[512,1,256]{2,0,1:T(8,128)(2,1)S(1)}, bf16[512,1,256]{2,0,1:T(8,128)(2,1)}, u32[]{:S(2)}) copy-start(bf16[512,1,256]{2,0,1:T(8,128)(2,1)} %param.5) | copy-start | bytes 786436
  1.6 0.9 %copy-start.1 = (bf16[1,128,768]{2,1,0:T(8,128)(2,1)S(1)}, bf16[1,128,768]{2,1,0:T(8,128)(2,1)}, u32[]{:S(2)}) copy-start(bf16[1,128,768]{2,1,0:T(8,128)(2,1)} %param.6) | copy-start | bytes 589828

commit v2 on v0

v2 whole, which is shorter than its diff:
```python
import jax
import jax.numpy as jnp
from jax import lax
from jax.experimental import pallas as pl
from jax.experimental.pallas import tpu as pltpu
from jax.sharding import PartitionSpec as P

BLOCK = 128
MESH = pl.DeviceIdType.MESH
NX, NY, NZH, NZL = 4, 8, 4, 3
HALF = 256
WIDE = 256
CHUNKS = 3
PARTS = 2

ORDERS = (
    (
        "up 0", "down 0", "own_x 0", "own_left 0", "up 1", "down 1", "own_left 1", "own_x 1",
        "own_x 2", "own_x 3", "own_x 4", "own_x 5", "X 0 0", "X 1 0", "X 2 0", "X 3 0",
        "Zp 0", "up 2", "X 4 0", "Zm 0", "down 2", "L 1 0", "X 5 0", "Zp 1",
        "up 3", "Zm 1", "down 3", "L 1 1", "X 0 1", "X 0 2", "Zo 0", "X 1 1",
        "L 2 0", "X 1 2", "Zp 2", "up 4", "Zm 2", "down 4", "X 0 3", "L 2 1",
        "Zo 1", "Zp 3", "up 5", "Zm 3", "down 5", "X 2 1", "X 2 2", "L 3 0",
        "X 1 3", "X 3 1", "Zp 4", "Zm 4", "X 3 2", "Zo 2", "L 3 1", "Zm 5",
        "Zp 5", "Zo 3", "X 4 1", "X 4 2", "X 2 3", "left_last", "x_last 0", "M 0",
        "X 5 2", "X 5 1", "Zo 4", "X 3 3", "R 0", "Zo 5", "x_last 1", "M 1",
        "X 4 3", "X 5 3", "R 1",
    ),
)


def kernel(
    left_hbm, right_hbm, left_flags, right_flags, target_flags, out_ref,
    left_in, right_in, left_buf, right_buf, part, sib_recv, red_send, red_recv,
    in_sem, left_send, left_recv, left_last, z_send, z_recv, x_send, x_recv, x_last,
    sib_send_sem, sib_recv_sem, red_send_sem, red_recv_sem,
):
    row, col, depth = lax.axis_index("row"), lax.axis_index("col"), lax.axis_index("depth")
    zh, x = row // NX, row % NX
    zl, core = depth // 2, depth % 2
    sign = 1 - 2 * core

    left_copy = pltpu.make_async_copy(left_hbm, left_in, in_sem.at[0])
    right_copy = pltpu.make_async_copy(right_hbm, right_in, in_sem.at[1])
    right_copy.start()
    left_copy.start()

    y_slot = {k: (col + k * sign + NY) % NY for k in range(-4, 4)}
    x_slot = {k: (x + k * sign + NX) % NX for k in (-1, 0, 1, 2)}
    zh_slot = {0: zh, 1: (zh + 3) % NZH, 2: (zh + 1) % NZH, 3: (zh + 2) % NZH}
    y_id = {k: (row, y_slot[k], depth) for k in (1, -1)}
    x_id = {k: (zh * NX + x_slot[k], col, depth) for k in (1, -1)}
    up_id = (zh_slot[2] * NX + x, col, depth)
    down_id = (zh_slot[1] * NX + x, col, depth)
    layer_id = {k: (row, col, ((zl + k) % NZL) * 2 + core) for k in (1, 2)}
    sibling = (row, col, zl * 2 + 1 - core)
    chunk = {k: (zl + 1 + k) % NZL for k in range(CHUNKS)}

    barrier = pltpu.get_barrier_semaphore()

    def greet(friend):
        pl.semaphore_signal(barrier, inc=1, device_id=friend, device_id_type=MESH)

    def mask_left():
        for block in range(4):
            rows = pl.ds(block * BLOCK, BLOCK)
            for k in range(2):
                columns = pl.ds(k * BLOCK, BLOCK)
                keep = left_flags[k, block] > 0
                value = left_in[rows, columns]
                left_buf[col, rows, columns] = jnp.where(keep, value, jnp.zeros_like(value))

    def mask_right(step):
        for j in range(2):
            keep = right_flags[0, chunk[step] * 2 + j] > 0
            start = pl.multiple_of(chunk[step] * WIDE + j * BLOCK, BLOCK)
            value = right_in[:, pl.ds(start, BLOCK)]
            right_buf[step, row, :, pl.ds(j * BLOCK, BLOCK)] = jnp.where(keep, value, jnp.zeros_like(value))

    def copy_of(ref, send_sem, recv_sem, target, dst=None):
        return pltpu.make_async_remote_copy(
            src_ref=ref, dst_ref=ref if dst is None else dst, send_sem=send_sem, recv_sem=recv_sem,
            device_id=target, device_id_type=MESH,
        )

    def left_copy_of(hop, way, half, shift):
        slot = y_slot[-shift] if way == 0 else y_slot[shift]
        final = hop == 4 - way
        return copy_of(
            left_buf.at[slot, pl.ds(half * HALF, HALF), :], left_send,
            left_last if final else left_recv.at[hop - 1, way, half], y_id[1 if way == 0 else -1],
        )

    def own_left(half):
        left_copy_of(1, 0, half, 0).start()
        left_copy_of(1, 1, half, 0).start()

    def left_event(hop, half):
        for way in range(2):
            if hop < 4 - way:
                left_copy_of(hop, way, half, hop).wait_recv()
                left_copy_of(hop + 1, way, half, hop).start()

    def z_copy(piece, source, arrival, target):
        rows = pl.ds(piece % PARTS * (BLOCK // PARTS), BLOCK // PARTS)
        ref = right_buf.at[piece // PARTS, zh_slot[source] * NX + x, rows]
        return copy_of(ref, z_send.at[piece // PARTS], z_recv.at[piece, arrival], target)

    def up(piece):
        z_copy(piece, 0, 0, up_id).start()

    def down(piece):
        z_copy(piece, 0, 1, down_id).start()

    def z_from_before(piece):
        z_copy(piece, 1, 0, up_id).wait_recv()

        @pl.when(core == 0)
        def _():
            z_copy(piece, 1, 2, up_id).start()

        own_x(piece, 1)

    def z_from_after(piece):
        z_copy(piece, 2, 1, down_id).wait_recv()

        @pl.when(core == 1)
        def _():
            z_copy(piece, 2, 2, down_id).start()

        own_x(piece, 2)

    def z_opposite(piece):
        z_copy(piece, 3, 2, up_id).wait_recv()
        own_x(piece, 3)

    def x_copy(piece, source, shift, recv_sem, way):
        rows = pl.ds(piece % PARTS * (BLOCK // PARTS), BLOCK // PARTS)
        ref = right_buf.at[piece // PARTS, zh_slot[source] * NX + x_slot[shift], rows]
        return copy_of(ref, x_send.at[piece // PARTS], recv_sem, x_id[way])

    def own_x(piece, source=0):
        x_copy(piece, source, 0, x_recv.at[piece, source], 1).start()
        x_copy(piece, source, 0, x_last.at[piece // PARTS], -1).start()

    def x_event(piece, source):
        x_copy(piece, source, -1, x_recv.at[piece, source], 1).wait_recv()
        x_copy(piece, source, -1, x_last.at[piece // PARTS], 1).start()

    def wait_x_last(step):
        blocks = right_buf.at[step, pl.ds(0, 8)]
        copy_of(blocks, x_send.at[step], x_last.at[step], x_id[1]).wait_recv()

    def wait_left_last():
        copy_of(left_buf.at[pl.ds(0, 2)], left_send, left_last, y_id[1]).wait_recv()

    def sibling_copy(step):
        return copy_of(part.at[step, 1 - core], sib_send_sem.at[step], sib_recv_sem.at[step], sibling, sib_recv.at[step])

    def layer_copy(step):
        return copy_of(red_send.at[step], red_send_sem.at[step], red_recv_sem.at[step], layer_id[1 + step], red_recv.at[step])

    def multiply(step):
        total = None
        for k in range(NY):
            term = jnp.dot(
                left_buf[k], right_buf[step, 2 * k:2 * k + 2].reshape(2 * BLOCK, WIDE),
                preferred_element_type=jnp.float32,
            )
            total = term if total is None else total + term
        part[step, 0] = total[:, :BLOCK]
        part[step, 1] = total[:, BLOCK:]
        sibling_copy(step).start()

    def reduce_send(step):
        sibling_copy(step).wait_recv()
        red_send[step] = part[step, core] + sib_recv[step]
        layer_copy(step).start()

    actions = {
        "own_x": own_x, "own_left": own_left, "X": x_event, "L": left_event, "up": up, "down": down, "Zp": z_from_before,
        "Zm": z_from_after, "Zo": z_opposite, "x_last": wait_x_last, "left_last": wait_left_last, "M": multiply,
        "R": reduce_send,
    }

    def perform(order):
        for item in order:
            name, *numbers = item.split()
            actions[name](*map(int, numbers))

    for friend in (y_id[1], y_id[-1], x_id[1], x_id[-1], sibling):
        greet(friend)
    right_copy.wait()
    for step in range(CHUNKS):
        mask_right(step)
    left_copy.wait()
    mask_left()
    for friend in (layer_id[1], layer_id[2], up_id, down_id):
        greet(friend)
    pl.semaphore_wait(barrier, 9)

    perform(ORDERS[0])

    copy_of(left_buf.at[pl.ds(0, 7)], left_send, left_last, y_id[1]).wait_send()
    for step in range(CHUNKS):
        copy_of(right_buf.at[step, pl.ds(0, 3)], z_send.at[step], z_recv.at[PARTS * step, 0], up_id).wait_send()
    for step in range(CHUNKS):
        copy_of(right_buf.at[step, pl.ds(0, 12)], x_send.at[step], x_last.at[step], x_id[1]).wait_send()
    wait_x_last(2)
    multiply(2)
    sibling_copy(0).wait_send()
    sibling_copy(1).wait_send()
    layer_copy(0).wait()
    layer_copy(1).wait()
    total = part[2, core] + red_recv[0] + red_recv[1]
    sibling_copy(2).wait()
    total = total + sib_recv[2]
    for block in range(4):
        rows = slice(block * BLOCK, (block + 1) * BLOCK)
        keep = target_flags[0, block] > 0
        value = total[rows]
        out_ref[rows, :] = jnp.where(keep, value, jnp.zeros_like(value)).astype(jnp.bfloat16)


def on_device(left_panels, right_panels, left_flags, right_flags, target_flags):
    dma = pltpu.SemaphoreType.DMA
    return pl.pallas_call(
        kernel,
        out_shape=jax.ShapeDtypeStruct((4 * BLOCK, BLOCK), jnp.bfloat16),
        in_specs=[pl.BlockSpec(memory_space=pl.ANY)] * 2 + [pl.BlockSpec(memory_space=pltpu.SMEM)] * 3,
        out_specs=pl.BlockSpec(memory_space=pltpu.VMEM),
        scratch_shapes=[
            pltpu.VMEM((4 * BLOCK, 2 * BLOCK), jnp.bfloat16),
            pltpu.VMEM((BLOCK, 6 * BLOCK), jnp.bfloat16),
            pltpu.VMEM((NY, 4 * BLOCK, 2 * BLOCK), jnp.bfloat16),
            pltpu.VMEM((CHUNKS, NX * NZH, BLOCK, WIDE), jnp.bfloat16),
            pltpu.VMEM((CHUNKS, 2, 4 * BLOCK, BLOCK), jnp.float32),
            pltpu.VMEM((CHUNKS, 4 * BLOCK, BLOCK), jnp.float32),
            pltpu.VMEM((2, 4 * BLOCK, BLOCK), jnp.float32),
            pltpu.VMEM((2, 4 * BLOCK, BLOCK), jnp.float32),
            dma((2,)),
            dma,
            dma((3, 2, 2)),
            dma,
            dma((CHUNKS,)),
            dma((CHUNKS * PARTS, 3)),
            dma((CHUNKS,)),
            dma((CHUNKS * PARTS, 4)),
            dma((CHUNKS,)),
            dma((CHUNKS,)),
            dma((CHUNKS,)),
            dma((2,)),
            dma((2,)),
        ],
        compiler_params=pltpu.CompilerParams(
            collective_id=0, has_side_effects=True, vmem_limit_bytes=VMEM_LIMIT
        ),
        cost_estimate=pl.CostEstimate(flops=1_610_612_736, bytes_accessed=600_000, transcendentals=0),
    )(left_panels[:, 0, :], right_panels[0], left_flags[:, 0, :].T, right_flags[0], target_flags.T)


VMEM_LIMIT = 63 * 1024 * 1024


def solution(mesh):
    in_specs = (
        P("row", "depth", "col"),
        P("depth", "row", "col"),
        P("row", "depth", "col"),
        P("depth", "row", "col"),
        P("row", ("col", "depth")),
    )
    out_specs = P("row", ("col", "depth"))
    return jax.shard_map(
        on_device, mesh=mesh, in_specs=in_specs, out_specs=out_specs, check_vma=False
    )
```

time: 218 us -> 63.3 us (0.29)
  waiting for transfers between devices: 191 us -> 0 us
  Pallas kernels: 0 us -> 61.5 us
  between operations: 13.1 us -> 0.01 us
  other arithmetic: 6.42 us -> 0 us
  matrix products: 5.53 us -> 0 us
    all_gather x2 -> x0, waiting for transfers between devices: 158 us -> none  [the longest x1 104 us: on_device(): gathered_right = lax.all_gather(right_masked, 'row', axis=0, tiled=True)]
    pallas_call x0 -> x1, Pallas kernels: none -> 61.5 us  [on_device(): pl.pallas_call(kernel, out_shape=jax.ShapeDtypeStruct((4 * BLOCK, BLOCK),...]
    reduce_scatter x1 -> x0, waiting for transfers between devices: 32.5 us -> none  [on_device(): lax.psum_scatter(partial_value, 'depth', scatter_dimension=1, tiled=True)]
    dot_general x1 -> x0, matrix products: 5.53 us -> none  [on_device(): jnp.dot(lax.all_gather(left_masked, 'col', axis=1, tiled=True), gathered_...]
    mul x2 -> x0, other arithmetic: 3.33 us -> none  [the longest x1 1.7 us: on_device(): left_panels[:, 0, :] * spread(left_flags[:, 0, :], jnp.bfloat16)]
    convert_element_type x4 -> x0, other arithmetic: 3.09 us -> none  [the longest x1 1.74 us: on_device(): return (summed * spread(target_flags, jnp.float32)).astype(jnp.bfloat16)]
  transfers between devices with their start and end apart: 3 -> 0, of which waited for: 3 -> 0; matrix products, arithmetic and copies ran while one was open for 1% -> 0% of each run, Pallas kernels for 0% -> 0%
where the time goes in v2:
time: 63.3 us; the launch traced here: 63.1 us
  Pallas kernels  61.5 us (97%)
  local copies, waits for them, and re-layouts  1.57 us (2%)
    pallas_call x1, Pallas kernels, on_device(): pl.pallas_call(kernel, out_shape=jax.ShapeDtypeStruct((4 * BLOCK, BLOCK),...  61.5 us
    unnamed x1, local copies, waits for them, and re-layouts  1.57 us

profile of v2, /device:TPU:1, one launch (start us, length us, event | category | flops | bytes accessed | tf_op | source)
XLA Modules:
  0.0 63.1 jit_solution(2959901504874507459)
XLA Ops:
  0.0 61.5 %shard_map.55 = bf16[512,128]{1,0:T(8,128)(2,1)} custom-call(bf16[512,256]{1,0:T(8,128)(2,1)} %bitcast.7, bf16[128,768]{1,0:T(8,128)(2,1)} %bitcast.8, s32[2,4]{1,0:T(2,128)} %bitcast.9, s32[1,6]{1,0:T(1,128)} %bitcast.10, s32[1,4]{1,0:T(1,128)} %bitcast.11), custom_call_target="tpu_custom_call" | custom-call | flops 1610612736 | bytes 600000 | tf_op jit(solution)/shard_map/pallas_call | solution.py:227
  61.6 1.6 %copy.7 = bf16[512,128]{1,0:T(8,128)(2,1)} copy(bf16[512,128]{1,0:T(8,128)(2,1)} %shard_map.55) | data formatting | bytes 262144

commit v3 on v2

--- a/solution.py
+++ b/solution.py
@@ -19,18 +19,19 @@
         "own_x 2", "own_x 3", "own_x 4", "own_x 5", "X 0 0", "X 1 0", "X 2 0", "X 3 0",
         "Zp 0", "up 2", "X 4 0", "Zm 0", "down 2", "L 1 0", "X 5 0", "Zp 1",
         "up 3", "Zm 1", "down 3", "L 1 1", "X 0 1", "X 0 2", "Zo 0", "X 1 1",
-        "L 2 0", "X 1 2", "Zp 2", "up 4", "Zm 2", "down 4", "X 0 3", "L 2 1",
-        "Zo 1", "Zp 3", "up 5", "Zm 3", "down 5", "X 2 1", "X 2 2", "L 3 0",
-        "X 1 3", "X 3 1", "Zp 4", "Zm 4", "X 3 2", "Zo 2", "L 3 1", "Zm 5",
-        "Zp 5", "Zo 3", "X 4 1", "X 4 2", "X 2 3", "left_last", "x_last 0", "M 0",
-        "X 5 2", "X 5 1", "Zo 4", "X 3 3", "R 0", "Zo 5", "x_last 1", "M 1",
+        "L 2 0", "X 1 2", "Zp 2", "Zo 1", "Zm 2", "up 4", "down 4", "X 0 3",
+        "L 2 1", "Zp 3", "up 5", "Zm 3", "down 5", "X 2 1", "X 2 2", "L 3 0",
+        "X 1 3", "X 3 1", "Zp 4", "Zm 4", "Zo 3", "X 3 2", "L 3 1", "Zm 5",
+        "Zo 2", "Zp 5", "X 4 1", "X 4 2", "X 2 3", "left_last", "x_last 0", "M 0",
+        "Zo 4", "X 5 2", "X 5 1", "X 3 3", "R 0", "x_last 1", "M 1", "Zo 5",
         "X 4 3", "X 5 3", "R 1",
     ),
 )
 
 
 def kernel(
-    left_hbm, right_hbm, left_flags, right_flags, target_flags, out_ref,
+    left_hbm, right_hbm, left_flags_hbm, right_flags_hbm, target_flags_hbm, out_ref,
+    left_flags, right_flags, target_flags,
     left_in, right_in, left_buf, right_buf, part, sib_recv, red_send, red_recv,
     in_sem, left_send, left_recv, left_last, z_send, z_recv, x_send, x_recv, x_last,
     sib_send_sem, sib_recv_sem, red_send_sem, red_recv_sem,
@@ -42,8 +43,16 @@
 
     left_copy = pltpu.make_async_copy(left_hbm, left_in, in_sem.at[0])
     right_copy = pltpu.make_async_copy(right_hbm, right_in, in_sem.at[1])
+    flag_copies = [
+        pltpu.make_async_copy(right_flags_hbm, right_flags, in_sem.at[2]),
+        pltpu.make_async_copy(left_flags_hbm, left_flags, in_sem.at[3]),
+        pltpu.make_async_copy(target_flags_hbm, target_flags, in_sem.at[4]),
+    ]
     right_copy.start()
+    flag_copies[0].start()
     left_copy.start()
+    flag_copies[1].start()
+    flag_copies[2].start()
 
     y_slot = {k: (col + k * sign + NY) % NY for k in range(-4, 4)}
     x_slot = {k: (x + k * sign + NX) % NX for k in (-1, 0, 1, 2)}
@@ -191,9 +200,12 @@
     for friend in (y_id[1], y_id[-1], x_id[1], x_id[-1], sibling):
         greet(friend)
     right_copy.wait()
+    flag_copies[0].wait()
     for step in range(CHUNKS):
         mask_right(step)
     left_copy.wait()
+    flag_copies[1].wait()
+    flag_copies[2].wait()
     mask_left()
     for friend in (layer_id[1], layer_id[2], up_id, down_id):
         greet(friend)
@@ -227,9 +239,12 @@
     return pl.pallas_call(
         kernel,
         out_shape=jax.ShapeDtypeStruct((4 * BLOCK, BLOCK), jnp.bfloat16),
-        in_specs=[pl.BlockSpec(memory_space=pl.ANY)] * 2 + [pl.BlockSpec(memory_space=pltpu.SMEM)] * 3,
+        in_specs=[pl.BlockSpec(memory_space=pl.ANY)] * 5,
         out_specs=pl.BlockSpec(memory_space=pltpu.VMEM),
         scratch_shapes=[
+            pltpu.SMEM((2, 4), jnp.int32),
+            pltpu.SMEM((1, 6), jnp.int32),
+            pltpu.SMEM((1, 4), jnp.int32),
             pltpu.VMEM((4 * BLOCK, 2 * BLOCK), jnp.bfloat16),
             pltpu.VMEM((BLOCK, 6 * BLOCK), jnp.bfloat16),
             pltpu.VMEM((NY, 4 * BLOCK, 2 * BLOCK), jnp.bfloat16),
@@ -238,7 +253,7 @@
             pltpu.VMEM((CHUNKS, 4 * BLOCK, BLOCK), jnp.float32),
             pltpu.VMEM((2, 4 * BLOCK, BLOCK), jnp.float32),
             pltpu.VMEM((2, 4 * BLOCK, BLOCK), jnp.float32),
-            dma((2,)),
+            dma((5,)),
             dma,
             dma((3, 2, 2)),
             dma,

time: 63.3 us -> 61.7 us (0.975); the launches traced: 63.1 us -> 60.9 us
  Pallas kernels: 61.5 us -> 59.3 us
    pallas_call x1, Pallas kernels: 61.5 us -> 59.3 us  [on_device(): pl.pallas_call(kernel, out_shape=jax.ShapeDtypeStruct((4 * BLOCK, BLOCK),...]
where the time goes in v3:
time: 61.7 us; the launch traced here: 60.9 us
  Pallas kernels  59.3 us (96%)
  local copies, waits for them, and re-layouts  1.57 us (3%)
    pallas_call x1, Pallas kernels, on_device(): pl.pallas_call(kernel, out_shape=jax.ShapeDtypeStruct((4 * BLOCK, BLOCK),...  59.3 us
    unnamed x1, local copies, waits for them, and re-layouts  1.57 us

profile of v3, /device:TPU:1, one launch (start us, length us, event | category | flops | bytes accessed | tf_op | source)
XLA Modules:
  0.0 60.9 jit_solution(13194795973937891285)
XLA Ops:
  0.0 59.3 %shard_map.55 = bf16[512,128]{1,0:T(8,128)(2,1)} custom-call(bf16[512,256]{1,0:T(8,128)(2,1)} %bitcast.7, bf16[128,768]{1,0:T(8,128)(2,1)} %bitcast.8, s32[2,4]{1,0:T(2,128)} %bitcast.9, s32[1,6]{1,0:T(1,128)} %bitcast.10, s32[1,4]{1,0:T(1,128)} %bitcast.11), custom_call_target="tpu_custom_call" | custom-call | flops 1610612736 | bytes 600000 | tf_op jit(solution)/shard_map/pallas_call | solution.py:239
  59.3 1.6 %copy.7 = bf16[512,128]{1,0:T(8,128)(2,1)} copy(bf16[512,128]{1,0:T(8,128)(2,1)} %shard_map.55) | data formatting | bytes 262144

commit v4 on v3

--- a/solution.py
+++ b/solution.py
@@ -18,13 +18,13 @@
         "up 0", "down 0", "own_x 0", "own_left 0", "up 1", "down 1", "own_left 1", "own_x 1",
         "own_x 2", "own_x 3", "own_x 4", "own_x 5", "X 0 0", "X 1 0", "X 2 0", "X 3 0",
         "Zp 0", "up 2", "X 4 0", "Zm 0", "down 2", "L 1 0", "X 5 0", "Zp 1",
-        "up 3", "Zm 1", "down 3", "L 1 1", "X 0 1", "X 0 2", "Zo 0", "X 1 1",
-        "L 2 0", "X 1 2", "Zp 2", "Zo 1", "Zm 2", "up 4", "down 4", "X 0 3",
-        "L 2 1", "Zp 3", "up 5", "Zm 3", "down 5", "X 2 1", "X 2 2", "L 3 0",
-        "X 1 3", "X 3 1", "Zp 4", "Zm 4", "Zo 3", "X 3 2", "L 3 1", "Zm 5",
-        "Zo 2", "Zp 5", "X 4 1", "X 4 2", "X 2 3", "left_last", "x_last 0", "M 0",
-        "Zo 4", "X 5 2", "X 5 1", "X 3 3", "R 0", "x_last 1", "M 1", "Zo 5",
-        "X 4 3", "X 5 3", "R 1",
+        "up 3", "Zm 1", "down 3", "L 1 1", "X 0 1", "X 0 2", "X 1 1", "L 2 0",
+        "Zo 0", "X 1 2", "Zp 2", "Zo 1", "Zm 2", "up 4", "down 4", "X 0 3",
+        "L 2 1", "Zp 3", "up 5", "Zm 3", "down 5", "X 2 1", "X 2 2", "X 1 3",
+        "L 3 0", "X 3 1", "Zp 4", "Zm 4", "Zo 3", "X 3 2", "L 3 1", "Zo 2",
+        "Zp 5", "X 4 1", "Zm 5", "X 4 2", "x_last 0", "X 2 3", "left_last", "M 0",
+        "Zo 4", "X 5 2", "X 5 1", "X 3 3", "R 0", "x_last 1", "M 1", "X 4 3",
+        "Zo 5", "X 5 3", "R 1",
     ),
 )
 
@@ -169,7 +169,7 @@
     def layer_copy(step):
         return copy_of(red_send.at[step], red_send_sem.at[step], red_recv_sem.at[step], layer_id[1 + step], red_recv.at[step])
 
-    def multiply(step):
+    def multiply_whole(step):
         total = None
         for k in range(NY):
             term = jnp.dot(
@@ -180,6 +180,24 @@
         part[step, 0] = total[:, :BLOCK]
         part[step, 1] = total[:, BLOCK:]
         sibling_copy(step).start()
+
+    def multiply_half(step, half):
+        columns = pl.ds(pl.multiple_of(half * BLOCK, BLOCK), BLOCK)
+        total = None
+        for k in range(NY):
+            term = jnp.dot(
+                left_buf[k], right_buf[step, 2 * k:2 * k + 2, :, columns].reshape(2 * BLOCK, BLOCK),
+                preferred_element_type=jnp.float32,
+            )
+            total = term if total is None else total + term
+        part[step, half] = total
+
+    def multiply(step):
+        if step < 2:
+            return multiply_whole(step)
+        multiply_half(step, 1 - core)
+        sibling_copy(step).start()
+        multiply_half(step, core)
 
     def reduce_send(step):
         sibling_copy(step).wait_recv()

time: 61.7 us -> 62.1 us (level)
  Pallas kernels: 59.3 us -> 60.2 us
    pallas_call x1, Pallas kernels: 59.3 us -> 60.2 us  [on_device(): pl.pallas_call(kernel, out_shape=jax.ShapeDtypeStruct((4 * BLOCK, BLOCK),...]
where the time goes in v4:
time: 62.1 us; the launch traced here: 61.8 us
  Pallas kernels  60.2 us (97%)
  local copies, waits for them, and re-layouts  1.57 us (3%)
    pallas_call x1, Pallas kernels, on_device(): pl.pallas_call(kernel, out_shape=jax.ShapeDtypeStruct((4 * BLOCK, BLOCK),...  60.2 us
    unnamed x1, local copies, waits for them, and re-layouts  1.57 us

profile of v4, /device:TPU:1, one launch (start us, length us, event | category | flops | bytes accessed | tf_op | source)
XLA Modules:
  0.0 61.8 jit_solution(15394170970938313246)
XLA Ops:
  0.0 60.2 %shard_map.55 = bf16[512,128]{1,0:T(8,128)(2,1)} custom-call(bf16[512,256]{1,0:T(8,128)(2,1)} %bitcast.7, bf16[128,768]{1,0:T(8,128)(2,1)} %bitcast.8, s32[2,4]{1,0:T(2,128)} %bitcast.9, s32[1,6]{1,0:T(1,128)} %bitcast.10, s32[1,4]{1,0:T(1,128)} %bitcast.11), custom_call_target="tpu_custom_call" | custom-call | flops 1610612736 | bytes 600000 | tf_op jit(solution)/shard_map/pallas_call | solution.py:257
  60.2 1.6 %copy.7 = bf16[512,128]{1,0:T(8,128)(2,1)} copy(bf16[512,128]{1,0:T(8,128)(2,1)} %shard_map.55) | data formatting | bytes 262144

commit v5 on v3

--- a/solution.py
+++ b/solution.py
@@ -18,13 +18,13 @@
         "up 0", "down 0", "own_x 0", "own_left 0", "up 1", "down 1", "own_left 1", "own_x 1",
         "own_x 2", "own_x 3", "own_x 4", "own_x 5", "X 0 0", "X 1 0", "X 2 0", "X 3 0",
         "Zp 0", "up 2", "X 4 0", "Zm 0", "down 2", "L 1 0", "X 5 0", "Zp 1",
-        "up 3", "Zm 1", "down 3", "L 1 1", "X 0 1", "X 0 2", "Zo 0", "X 1 1",
-        "L 2 0", "X 1 2", "Zp 2", "Zo 1", "Zm 2", "up 4", "down 4", "X 0 3",
-        "L 2 1", "Zp 3", "up 5", "Zm 3", "down 5", "X 2 1", "X 2 2", "L 3 0",
-        "X 1 3", "X 3 1", "Zp 4", "Zm 4", "Zo 3", "X 3 2", "L 3 1", "Zm 5",
-        "Zo 2", "Zp 5", "X 4 1", "X 4 2", "X 2 3", "left_last", "x_last 0", "M 0",
-        "Zo 4", "X 5 2", "X 5 1", "X 3 3", "R 0", "x_last 1", "M 1", "Zo 5",
-        "X 4 3", "X 5 3", "R 1",
+        "up 3", "Zm 1", "down 3", "L 1 1", "X 0 1", "X 0 2", "X 1 1", "L 2 0",
+        "Zo 0", "X 1 2", "Zp 2", "Zo 1", "Zm 2", "up 4", "down 4", "X 0 3",
+        "L 2 1", "Zp 3", "up 5", "Zm 3", "down 5", "X 2 1", "X 2 2", "X 1 3",
+        "L 3 0", "X 3 1", "Zp 4", "Zm 4", "Zo 3", "X 3 2", "L 3 1", "Zo 2",
+        "Zp 5", "X 4 1", "Zm 5", "X 4 2", "x_last 0", "X 2 3", "left_last", "M 0",
+        "Zo 4", "X 5 2", "X 5 1", "X 3 3", "R 0", "x_last 1", "M 1", "X 4 3",
+        "Zo 5", "X 5 3", "R 1",
     ),
 )
 

time: 61.7 us -> 61.6 us (level)
  no operation moved by 1% of the time
where the time goes in v5:
time: 61.6 us; the launch traced here: 61.2 us
  Pallas kernels  59.7 us (97%)
  local copies, waits for them, and re-layouts  1.57 us (3%)
    pallas_call x1, Pallas kernels, on_device(): pl.pallas_call(kernel, out_shape=jax.ShapeDtypeStruct((4 * BLOCK, BLOCK),...  59.7 us
    unnamed x1, local copies, waits for them, and re-layouts  1.57 us

profile of v5, /device:TPU:1, one launch (start us, length us, event | category | flops | bytes accessed | tf_op | source)
XLA Modules:
  0.0 61.2 jit_solution(14982347375662296928)
XLA Ops:
  0.0 59.7 %shard_map.55 = bf16[512,128]{1,0:T(8,128)(2,1)} custom-call(bf16[512,256]{1,0:T(8,128)(2,1)} %bitcast.7, bf16[128,768]{1,0:T(8,128)(2,1)} %bitcast.8, s32[2,4]{1,0:T(2,128)} %bitcast.9, s32[1,6]{1,0:T(1,128)} %bitcast.10, s32[1,4]{1,0:T(1,128)} %bitcast.11), custom_call_target="tpu_custom_call" | custom-call | flops 1610612736 | bytes 600000 | tf_op jit(solution)/shard_map/pallas_call | solution.py:239
  59.7 1.6 %copy.7 = bf16[512,128]{1,0:T(8,128)(2,1)} copy(bf16[512,128]{1,0:T(8,128)(2,1)} %shard_map.55) | data formatting | bytes 262144

commit v6 on v5

--- a/solution.py
+++ b/solution.py
@@ -15,16 +15,16 @@
 
 ORDERS = (
     (
-        "up 0", "down 0", "own_x 0", "own_left 0", "up 1", "down 1", "own_left 1", "own_x 1",
-        "own_x 2", "own_x 3", "own_x 4", "own_x 5", "X 0 0", "X 1 0", "X 2 0", "X 3 0",
-        "Zp 0", "up 2", "X 4 0", "Zm 0", "down 2", "L 1 0", "X 5 0", "Zp 1",
-        "up 3", "Zm 1", "down 3", "L 1 1", "X 0 1", "X 0 2", "X 1 1", "L 2 0",
-        "Zo 0", "X 1 2", "Zp 2", "Zo 1", "Zm 2", "up 4", "down 4", "X 0 3",
-        "L 2 1", "Zp 3", "up 5", "Zm 3", "down 5", "X 2 1", "X 2 2", "X 1 3",
-        "L 3 0", "X 3 1", "Zp 4", "Zm 4", "Zo 3", "X 3 2", "L 3 1", "Zo 2",
-        "Zp 5", "X 4 1", "Zm 5", "X 4 2", "x_last 0", "X 2 3", "left_last", "M 0",
-        "Zo 4", "X 5 2", "X 5 1", "X 3 3", "R 0", "x_last 1", "M 1", "X 4 3",
-        "Zo 5", "X 5 3", "R 1",
+        "up 0", "down 0", "own_x 0", "up 1", "down 1", "own_x 1", "ready_left", "own_left 0",
+        "own_left 1", "ready_right", "own_x 2", "own_x 3", "own_x 4", "own_x 5", "X 0 0", "X 1 0",
+        "X 2 0", "X 3 0", "Zp 0", "up 2", "X 4 0", "Zm 0", "down 2", "L 1 0",
+        "X 5 0", "Zp 1", "up 3", "Zm 1", "down 3", "L 1 1", "X 0 1", "X 0 2",
+        "X 1 1", "L 2 0", "Zo 0", "X 1 2", "Zp 2", "Zo 1", "Zm 2", "up 4",
+        "down 4", "X 0 3", "L 2 1", "Zp 3", "up 5", "Zm 3", "down 5", "X 2 1",
+        "X 2 2", "X 1 3", "L 3 0", "X 3 1", "Zp 4", "Zm 4", "Zo 3", "X 3 2",
+        "L 3 1", "Zo 2", "Zp 5", "X 4 1", "Zm 5", "X 4 2", "x_last 0", "X 2 3",
+        "left_last", "M 0", "Zo 4", "X 5 2", "X 5 1", "X 3 3", "R 0", "x_last 1",
+        "M 1", "X 4 3", "Zo 5", "X 5 3", "R 1",
     ),
 )
 
@@ -186,7 +186,18 @@
         red_send[step] = part[step, core] + sib_recv[step]
         layer_copy(step).start()
 
+    def ready_left():
+        left_copy.wait()
+        flag_copies[1].wait()
+        flag_copies[2].wait()
+        mask_left()
+
+    def ready_right():
+        for step in range(1, CHUNKS):
+            mask_right(step)
+
     actions = {
+        "ready_left": ready_left, "ready_right": ready_right,
         "own_x": own_x, "own_left": own_left, "X": x_event, "L": left_event, "up": up, "down": down, "Zp": z_from_before,
         "Zm": z_from_after, "Zo": z_opposite, "x_last": wait_x_last, "left_last": wait_left_last, "M": multiply,
         "R": reduce_send,
@@ -201,12 +212,7 @@
         greet(friend)
     right_copy.wait()
     flag_copies[0].wait()
-    for step in range(CHUNKS):
-        mask_right(step)
-    left_copy.wait()
-    flag_copies[1].wait()
-    flag_copies[2].wait()
-    mask_left()
+    mask_right(0)
     for friend in (layer_id[1], layer_id[2], up_id, down_id):
         greet(friend)
     pl.semaphore_wait(barrier, 9)

time: 61.6 us -> 61.5 us (level)
  no operation moved by 1% of the time
where the time goes in v6:
time: 61.5 us; the launch traced here: 61.1 us
  Pallas kernels  59.6 us (97%)
  local copies, waits for them, and re-layouts  1.57 us (3%)
    pallas_call x1, Pallas kernels, on_device(): pl.pallas_call(kernel, out_shape=jax.ShapeDtypeStruct((4 * BLOCK, BLOCK),...  59.6 us
    unnamed x1, local copies, waits for them, and re-layouts  1.57 us

profile of v6, /device:TPU:1, one launch (start us, length us, event | category | flops | bytes accessed | tf_op | source)
XLA Modules:
  0.0 61.1 jit_solution(3226427540729605258)
XLA Ops:
  0.0 59.6 %shard_map.55 = bf16[512,128]{1,0:T(8,128)(2,1)} custom-call(bf16[512,256]{1,0:T(8,128)(2,1)} %bitcast.7, bf16[128,768]{1,0:T(8,128)(2,1)} %bitcast.8, s32[2,4]{1,0:T(2,128)} %bitcast.9, s32[1,6]{1,0:T(1,128)} %bitcast.10, s32[1,4]{1,0:T(1,128)} %bitcast.11), custom_call_target="tpu_custom_call" | custom-call | flops 1610612736 | bytes 600000 | tf_op jit(solution)/shard_map/pallas_call | solution.py:245
  59.6 1.6 %copy.7 = bf16[512,128]{1,0:T(8,128)(2,1)} copy(bf16[512,128]{1,0:T(8,128)(2,1)} %shard_map.55) | data formatting | bytes 262144
